TPU v7x, 128 devices: a whole 4x4x4 slice. The times are simulated.
128 devices in a mesh: sec: 4 (over y), dev: 32 (over z, x, core).
Axes of the slice: x: 4, y: 4, z: 4, core: 2. Of those that a mesh axis runs over, the one named last changes fastest.
Arguments:
- moe_input: bfloat16 [512, 7168], P(('sec', 'dev')), may hold values from -6 to 6
- expert_ids: int32 [512, 8], P(('sec', 'dev')), may hold values from 0 to 31, all different within a row; in each aligned block of 4 rows (0 to 3, 4 to 7, ...) at most 2 rows name the same one
- gate_weights: float32 [512, 8], P(('sec', 'dev')), may hold values from 0.1 to 0.6
- capacity: int32 [32], replicated, may hold values from 64 to 256
- gate_proj: bfloat16 [32, 7168, 2048], P('dev', None, 'sec'), may hold values from -0.0625 to 0.0625
- up_proj: bfloat16 [32, 7168, 2048], P('dev', None, 'sec'), may hold values from -0.0625 to 0.0625
- down_proj: bfloat16 [32, 2048, 7168], P('dev', 'sec'), may hold values from -0.125 to 0.125
- queries: bfloat16 [128, 128, 576], P(('sec', 'dev')), may hold values from -5 to 5
- latent_cache: bfloat16 [128, 2048, 576], P(('sec', 'dev')), may hold values from -5 to 5
- lengths: int32 [128], P(('sec', 'dev')), may hold values from 256 to 2048
Outputs:
- moe_output: bfloat16 [512, 7168], P(('sec', 'dev'))
- attn_output: bfloat16 [128, 128, 512], P(('sec', 'dev'))
Inputs may be any that keep to these rules, and one draw needn't show every extreme that they name: `expert_ids`: the 4 rows of one device name one expert at most 2 times; some device's rows name some expert exactly 2 times.
All inputs are finite; a program needn't handle non-finite values.
Results may differ from a plain program's by a relative error of at most 0.009.
Values may be sent and summed in bfloat16 or wider, within the bound.
A program may use at most 128 MiB of HBM per device.

v0:
```python
import jax
import jax.numpy as jnp
from jax import lax
from jax.sharding import PartitionSpec as P

LATENT = 512
SLOT = 2


softmax_scale = 192.0 ** (-0.5)


def entering(value, axis, join, neutral):
    count, mine = (lax.axis_size(axis), lax.axis_index(axis))
    pieces = lax.all_gather(value, axis)
    subtotal = jnp.full_like(value, 0) + jnp.asarray(neutral, value.dtype)

    def hop(position, subtotal):
        longer = join(subtotal, pieces[position])
        return jnp.where(position < mine, longer, subtotal)

    return lax.fori_loop(0, count - 1, hop, subtotal)


def attend_local(queries, latent_cache, lengths):
    scores = (
        jnp.einsum("shw,scw->shc", queries, latent_cache, preferred_element_type=jnp.float32)
        * softmax_scale
    )
    position = jnp.arange(latent_cache.shape[1], dtype=jnp.int32)
    scores = jnp.where(position[None, None, :] < lengths[:, None, None], scores, -jnp.inf)
    largest = jnp.max(scores, axis=2, keepdims=True)
    expo = jnp.exp(scores - largest)
    probs = (expo / jnp.sum(expo, axis=2, keepdims=True)).astype(jnp.bfloat16)
    values = latent_cache[:, :, :LATENT]
    return jnp.einsum("shc,scl->shl", probs, values, preferred_element_type=jnp.float32).astype(
        jnp.bfloat16
    )


def body(
    moe_input,
    expert_ids,
    gate_weights,
    capacity,
    gate_proj,
    up_proj,
    down_proj,
    queries,
    latent_cache,
    lengths,
):
    n_dev = lax.axis_size("dev")
    n_sec = lax.axis_size("sec")
    experts_all = capacity.shape[0]
    exp_local = gate_proj.shape[0]
    width = moe_input.shape[1]
    per_owner = exp_local * SLOT
    one_hot = (
        expert_ids[:, :, None] == jnp.arange(experts_all, dtype=jnp.int32)[None, None, :]
    ).astype(jnp.int32)
    row_counts = jnp.sum(one_hot, axis=1)
    dev_counts = jnp.sum(row_counts, axis=0)
    before_local = jnp.cumsum(row_counts, axis=0) - row_counts
    local_rank = jnp.sum(one_hot * before_local[:, None, :], axis=2)
    offsets = entering(
        dev_counts,
        ("sec", "dev"),
        lambda earlier, later: earlier + later,
        jnp.zeros_like(dev_counts),
    )
    arrival = local_rank + jnp.sum(one_hot * offsets[None, None, :], axis=2)
    limits = jnp.sum(one_hot * capacity[None, None, :], axis=2)
    kept_weight = jnp.where(arrival < limits, gate_weights, 0.0)
    slot_index = expert_ids * SLOT + local_rank
    placed = (
        slot_index[:, :, None] == jnp.arange(experts_all * SLOT, dtype=jnp.int32)[None, None, :]
    )
    picked = jnp.any(placed, axis=1).astype(jnp.bfloat16)
    combine_weight = jnp.sum(jnp.where(placed, kept_weight[:, :, None], 0.0), axis=1)
    outgoing = jnp.einsum(
        "ts,td->sd", picked, moe_input, preferred_element_type=jnp.float32
    ).astype(jnp.bfloat16)
    outgoing = outgoing.reshape(n_dev, per_owner, width)
    copies = jnp.broadcast_to(outgoing[None], (n_sec, n_dev, per_owner, width)).reshape(
        n_sec * n_dev, per_owner, width
    )
    arrived = lax.all_to_all(copies, ("sec", "dev"), split_axis=0, concat_axis=0, tiled=True)
    count = arrived.shape[0]
    grouped = arrived.reshape(count, exp_local, SLOT, width)
    gate_val = jnp.einsum("resd,edh->resh", grouped, gate_proj, preferred_element_type=jnp.float32)
    up_val = jnp.einsum("resd,edh->resh", grouped, up_proj, preferred_element_type=jnp.float32)
    hidden = (jax.nn.silu(gate_val) * up_val).astype(jnp.bfloat16)
    count = hidden.shape[0]
    result = jnp.einsum("resh,ehd->resd", hidden, down_proj, preferred_element_type=jnp.float32)
    partials = result.reshape(count, per_owner, width).astype(jnp.bfloat16)
    returned = lax.all_to_all(partials, ("sec", "dev"), split_axis=0, concat_axis=0, tiled=True)
    summed = jnp.sum(returned.reshape(n_sec, n_dev, per_owner, width).astype(jnp.float32), axis=0)
    expert_rows = summed.astype(jnp.bfloat16)
    flat_rows = expert_rows.reshape(experts_all * SLOT, width).astype(jnp.float32)
    mixed = jnp.dot(combine_weight, flat_rows, precision=lax.Precision.HIGHEST).astype(jnp.bfloat16)
    return (mixed, attend_local(queries, latent_cache, lengths))


def solution(mesh):
    placed = (
        P(("sec", "dev"), None),
        P(("sec", "dev"), None),
        P(("sec", "dev"), None),
        P(),
        P("dev", None, "sec"),
        P("dev", None, "sec"),
        P("dev", "sec", None),
        P(("sec", "dev"), None, None),
        P(("sec", "dev"), None, None),
        P(("sec", "dev")),
    )
    return jax.shard_map(
        body,
        mesh=mesh,
        in_specs=placed,
        out_specs=(P(("sec", "dev"), None), P(("sec", "dev"), None, None)),
        check_vma=False,
    )
```

profile of v0, /device:TPU:0, one launch (start us, length us, event | category | flops | bytes accessed | tf_op | source)
XLA Modules:
  0.0 208.3 jit_solution(17877033347857995930)
XLA Ops:
  0.6 0.0 copy-start
  0.7 0.8 convert_reduce_fusion
  1.5 0.3 dynamic-update-slice
  1.8 68.2 %all-reduce = s32[4096]{0:T(1024)S(1)} all-reduce(s32[4096]{0:T(1024)S(1)} %dynamic-update-slice), channel_id=2, replica_groups=mesh['sec'=4,'dev'=32] {'sec','dev'}, use_global_device_ids=true, to_apply=%add | all-reduce | flops 4096 | bytes 32768
  69.9 0.1 reshape.99
  70.0 5.1 %while.14 = (s32[]{:T(128)}, s32[32]{0:T(128)S(1)}, s32[]{:T(128)}, s32[128,32]{1,0:T(8,128)S(1)}, s32[]{:T(128)}, /*index=5*/s32[]{:T(128)}) while((s32[]{:T(128)}, s32[32]{0:T(128)S(1)}, s32[]{:T(128)}, s32[128,32]{1,0:T(8,128)S(1)}, s32[]{:T(128)}, /*index=5*/s32[]{:T(128)}) %tuple.40), condition=%wide.region_5.6_spmd.clone, body=%wide.region_4.5_spmd.clone.sunk | while | flops 100 | bytes 477 | solution.py:22
  75.2 1.0 select_reduce_fusion.2
  76.2 0.7 multiply_add_fusion
  76.9 0.1 fusion.47
  77.0 1.3 convolution_convert_fusion.1
  78.3 0.3 broadcast_in_dim.54
  78.6 1.9 broadcast_in_dim.55
  80.5 0.0 slice-start
  80.6 51.9 %all_to_all.10 = bf16[128,2,7168]{2,1,0:T(2,128)(2,1)S(1)} all-to-all(bf16[128,2,7168]{2,1,0:T(2,128)(2,1)S(1)} %bitcast.74), channel_id=1, replica_groups=mesh['sec'=4,'dev'=32] {'sec','dev'}, dimensions={0} | all-to-all | bytes 7340032 | tf_op jit(solution)/shard_map/all_to_all | solution.py:88
  132.4 5.3 %fusion.12 = f32[128,1,2,512]{3,0,2,1:T(8,128)S(1)} fusion(bf16[1,7168,512]{2,1,0:T(8,128)(2,1)} %param.16, bf16[128,2,7168]{2,1,0:T(2,128)(2,1)S(1)} %all_to_all.10), kind=kOutput, calls=%fused_computation.18 | convolution fusion | flops 1879048192 | bytes 11534336 | tf_op jit(solution)/shard_map/resd,edh->resh/dot_general | solution.py:91
  137.7 0.0 slice-done
  137.7 0.0 slice-done.1
  137.8 0.0 slice-start.3
  137.8 2.1 fusion.32
  139.8 0.0 slice-done.2
  139.9 0.0 slice-done.3
  139.9 2.2 %convolution_convert_fusion = bf16[128,2,7168]{2,0,1:T(8,128)(2,1)S(1)} fusion(bf16[128,2,512]{2,0,1:T(8,128)(2,1)S(1)} %fusion.32, bf16[1,512,7168]{2,1,0:T(8,128)(2,1)S(1)} %bitcast.78), kind=kOutput, calls=%fused_computation.2 | convolution fusion | flops 1880883200 | bytes 11272192 | tf_op jit(solution)/shard_map/resh,ehd->resd/dot_general | solution.py:95
  142.1 5.6 %copy.25 = bf16[128,2,7168]{2,1,0:T(2,128)(2,1)} copy(bf16[128,2,7168]{2,0,1:T(8,128)(2,1)S(1)} %convolution_convert_fusion) | data formatting | bytes 7340032 | tf_op jit(solution)/shard_map/convert_element_type | solution.py:96
  147.7 6.1 %all-to-all-start.1 = ((bf16[128,2,7168]{2,1,0:T(2,128)(2,1)}), bf16[128,2,7168]{2,1,0:T(2,128)(2,1)}, u32[]{:S(2)}, u32[]{:S(2)}) async-start(bf16[128,2,7168]{2,1,0:T(2,128)(2,1)} %copy.25), calls=%async_computation.1 | async-start | bytes 7340032 | tf_op jit(solution)/shard_map/all_to_all | solution.py:97
  154.5 0.1 select_reduce_fusion
  154.6 0.7 fusion.49
  155.3 0.3 fusion.43
  155.6 1.5 fusion.40
  157.1 43.3 %all-to-all-done.1 = bf16[128,2,7168]{2,1,0:T(2,128)(2,1)} async-done(((bf16[128,2,7168]{2,1,0:T(2,128)(2,1)}), bf16[128,2,7168]{2,1,0:T(2,128)(2,1)}, u32[]{:S(2)}, u32[]{:S(2)}) %all-to-all-start.1) | async-done | bytes 3670048 | tf_op jit(solution)/shard_map/all_to_all | solution.py:97
  200.4 6.4 %reduce_sum.81 = bf16[32,2,7168]{2,1,0:T(2,128)(2,1)S(1)} reduce(bf16[4,32,2,7168]{3,2,1,0:T(2,128)(2,1)} %bitcast.16, bf16[]{:T(256)} %constant.54.clone.1), dimensions={0}, to_apply=%region_10.11 | reduce | flops 1376256 | bytes 4587522 | tf_op jit(solution)/shard_map/reduce_sum | solution.py:98
  206.9 0.3 reshape.95
  207.2 1.1 convolution_convert_fusion.2
  (142 shorter events, 2.3 us)
Async XLA Ops:
  0.6 153.9 %copy-start = (bf16[1,128,576]{1,2,0:T(8,128)(2,1)S(1)}, bf16[1,128,576]{1,2,0:T(8,128)(2,1)}, u32[]{:S(2)}) copy-start(bf16[1,128,576]{1,2,0:T(8,128)(2,1)} %param.19) | copy-start | bytes 442372
  80.5 57.2 %slice-start = ((s8[7340032]{0:T(1024)(128)(4,1)}), s8[4194304]{0:T(1024)(128)(4,1)S(1)}, s32[]{:S(2)}) async-start(s8[7340032]{0:T(1024)(128)(4,1)} %bitcast.75), calls=%async_computation.2 | async-start | bytes 8388608
  132.4 5.3 %slice-start.1 = ((s8[7340032]{0:T(1024)(128)(4,1)}), s8[3145728]{0:T(1024)(128)(4,1)S(1)}, s32[]{:S(2)}) async-start(s8[7340032]{0:T(1024)(128)(4,1)} %bitcast.75), calls=%async_computation.3 | async-start | bytes 6291456
  132.4 7.4 %slice-start.2 = ((s8[7340032]{0:T(1024)(128)(4,1)}), s8[4194304]{0:T(1024)(128)(4,1)S(1)}, s32[]{:S(2)}) async-start(s8[7340032]{0:T(1024)(128)(4,1)} %bitcast.77), calls=%async_computation.4 | async-start | bytes 8388608
  137.8 2.1 %slice-start.3 = ((s8[7340032]{0:T(1024)(128)(4,1)}), s8[3145728]{0:T(1024)(128)(4,1)S(1)}, s32[]{:S(2)}) async-start(s8[7340032]{0:T(1024)(128)(4,1)} %bitcast.77), calls=%async_computation.5 | async-start | bytes 6291456
  147.7 6.8 %copy-start.2 = (f32[4,8]{1,0:T(4,128)S(1)}, f32[4,8]{1,0:T(4,128)}, u32[]{:S(2)}) copy-start(f32[4,8]{1,0:T(4,128)} %param.14) | copy-start | bytes 388
  147.7 6.9 %copy-start.1 = (bf16[1,2048,576]{1,2,0:T(8,128)(2,1)S(1)}, bf16[1,2048,576]{1,2,0:T(8,128)(2,1)}, u32[]{:S(2)}) copy-start(bf16[1,2048,576]{1,2,0:T(8,128)(2,1)} %param.20) | copy-start | bytes 7077892
  147.7 52.8 %all-to-all-start.1 = ((bf16[128,2,7168]{2,1,0:T(2,128)(2,1)}), bf16[128,2,7168]{2,1,0:T(2,128)(2,1)}, u32[]{:S(2)}, u32[]{:S(2)}) async-start(bf16[128,2,7168]{2,1,0:T(2,128)(2,1)} %copy.25), calls=%async_computation.1 | async-start | bytes 7340032 | tf_op jit(solution)/shard_map/all_to_all | solution.py:97
where the time goes:
time: 209 us; the launch traced here: 208 us
  blocking collectives  120 us (57%)
  waiting for transfers between devices  43.3 us (21%)
  matrix products  14.1 us (7%)
  other arithmetic  11.7 us (6%)
  local copies, waits for them, and re-layouts  8.58 us (4%)
  starting transfers between devices  6.1 us (3%)
  loops' own time  2.92 us (1%)
    unnamed x1, blocking collectives  68.2 us
    all_to_all x1, blocking collectives, body(): lax.all_to_all(copies, ('sec', 'dev'), split_axis=0, concat_axis=0, tiled...  51.9 us
    all_to_all x1, waiting for transfers between devices, body(): lax.all_to_all(partials, ('sec', 'dev'), split_axis=0, concat_axis=0, til...  43.3 us
    reduce_sum x1, other arithmetic, body(): jnp.sum(returned.reshape(n_sec, n_dev, per_owner, width).astype(jnp.float...  6.44 us
    all_to_all x1, starting transfers between devices, body(): lax.all_to_all(partials, ('sec', 'dev'), split_axis=0, concat_axis=0, til...  6.1 us
    convert_element_type x1, local copies, waits for them, and re-layouts, body(): partials = result.reshape(count, per_owner, width).astype(jnp.bfloat16)  5.61 us
    dot_general x1, matrix products, body(): jnp.einsum('resd,edh->resh', grouped, gate_proj, preferred_element_type=j...  5.28 us
  transfers between devices with their start and end apart: 1, of which 1 were waited for; matrix products, arithmetic and copies ran while one was open for 1% of the time, Pallas kernels for 0%

commit v1 on v0

v1 whole, which is shorter than its diff:
```python
import functools

import jax
import jax.numpy as jnp
from jax import lax
from jax.experimental import pallas as pl
from jax.experimental.pallas import tpu as pltpu
from jax.sharding import PartitionSpec as P

MESH = pl.DeviceIdType.MESH
BF16 = jnp.bfloat16
F32 = jnp.float32
LATENT = 512
D = 7168
HID = 512
HEADS = 128
CACHE = 2048
EXPERTS = 32
TOP = 8
LANE = 128
PART = 19 * LANE
FOLD = 5 * LANE
SUBS = ((0, 10), (10, 9))
NSUB = len(SUBS)
ORDERS = ("xyz", "yzx", "zxy")
SCALE = 192.0 ** (-0.5)


def span(p, s):
    off, count = SUBS[s]
    skip = LANE if (p == 2 and s == 0) else 0
    start = p * PART + off * LANE + skip - (LANE if p == 2 else 0)
    return skip, count * LANE - skip, start


def mm(a, b):
    return jnp.dot(a, b, preferred_element_type=F32)


def nt(a, b):
    return lax.dot_general(a, b, (((1,), (1,)), ((), ())), preferred_element_type=F32)


def tn(a, b):
    return lax.dot_general(a, b, (((0,), (0,)), ((), ())), preferred_element_type=F32)


def axes_of(i, p):
    a = {ORDERS[p][2]: (i >> 6) & 3, ORDERS[p][1]: (i >> 4) & 3, ORDERS[p][0]: (i >> 2) & 3}
    return a["x"], a["y"], a["z"], (i >> 8) & 1, i & 3


def token_of(i, p):
    x, y, z, c, r = axes_of(i, p)
    return y * 128 + z * 32 + x * 8 + c * 4 + r


def place_of(i, p):
    x, y, z, _, _ = axes_of(i, p)
    return y * 16 + x * 4 + z


def kernel(
    lengths_ref, capacity_ref, x_ref, ids_ref, gw_ref, q_hbm, kv_hbm, gate_hbm, up_hbm, down_hbm,
    out_ref, attn_ref,
    q, kv, gate, up, down, scores, probs,
    fold, s1, xb, sel, kept_col, packed, acc_g, acc_u, ht,
    cs, cr, rv, us, rw, vq, d3, r3,
    lsem, s1_sem, g2_sem, g3_sem, cx_sem, r0_sem, r1_sem, r2_sem, r3_sem,
):
    y = lax.axis_index("sec")
    dev = lax.axis_index("dev")
    z, x, c = dev // 8, (dev // 2) % 4, dev % 2
    at = {"x": x, "y": y, "z": z}

    def peer(axis, step):
        to = dict(at)
        to[axis] = (at[axis] + step + 4) % 4
        return (to["y"], to["z"] * 8 + to["x"] * 2 + c)

    sibling = (y, z * 8 + x * 2 + (1 - c))
    barrier = pltpu.get_barrier_semaphore()
    for axis in "xyz":
        for step in (1, 2, 3):
            pl.semaphore_signal(barrier, inc=1, device_id=peer(axis, step), device_id_type=MESH)
    pl.semaphore_signal(barrier, inc=1, device_id=sibling, device_id_type=MESH)

    local = {}
    for n, (src, dst) in enumerate(
        ((q_hbm.at[0], q), (kv_hbm.at[0], kv), (gate_hbm.at[0], gate), (up_hbm.at[0], up), (down_hbm.at[0], down))
    ):
        local[n] = pltpu.make_async_copy(src, dst, lsem.at[n])
        local[n].start()

    sent = {}

    def send(key, sems, index, src, dst, to):
        copy = pltpu.make_async_remote_copy(
            src_ref=src, dst_ref=dst,
            send_sem=sems.at[(0,) + index], recv_sem=sems.at[(1,) + index],
            device_id=to, device_id_type=MESH,
        )
        copy.start()
        sent[key] = copy

    def got(key):
        sent[key].wait_recv()

    lane = lax.broadcasted_iota(jnp.int32, (4, LANE), 1)
    info = jnp.zeros((4, LANE), F32)
    ids = ids_ref[...]
    gw = gw_ref[...]
    high = gw.astype(BF16).astype(F32)
    mid = (gw - high).astype(BF16).astype(F32)
    low = gw - high - mid
    for k in range(TOP):
        for n, piece in enumerate((high, mid, low)):
            info = info + jnp.where(lane == ids[:, k:k + 1] + n * EXPERTS, piece[:, k:k + 1], 0.0)
    fold[...] = jnp.zeros_like(fold)
    for p in range(3):
        for f in range(4):
            first, width = f * FOLD, min(FOLD, PART - f * FOLD)
            lead = LANE if (p == 2 and f == 0) else 0
            start = p * PART + first + lead - (LANE if p == 2 else 0)
            fold[p, 4 * f:4 * f + 4, lead:width] = x_ref[:, start:start + width - lead].astype(F32)
    fold[2, 0:4, 0:LANE] = info
    for p in range(3):
        s1[p, at[ORDERS[p][0]]] = fold[p].astype(BF16)
    pl.semaphore_wait(barrier, 10)
    for step in (1, 2, 3):
        for p in range(3):
            axis = ORDERS[p][0]
            mine = s1.at[p, at[axis]]
            send(("s1", p, step), s1_sem, (p, step - 1), mine, mine, peer(axis, step))

    def attend_scores():
        local[0].wait()
        local[1].wait()
        position = lax.broadcasted_iota(jnp.int32, (1, 512), 1)
        length = lengths_ref[0]
        for n in range(CACHE // 512):
            rows = kv[n * 512:(n + 1) * 512, :]
            score = nt(q[:, :LATENT], rows[:, :LATENT]) + nt(q[:, LATENT:], rows[:, LATENT:])
            scores[:, n * 512:(n + 1) * 512] = jnp.where(position + n * 512 < length, score * SCALE, -jnp.inf)

    def attend_probs():
        score = scores[...]
        expo = jnp.exp(score - jnp.max(score, axis=1, keepdims=True))
        probs[...] = (expo / jnp.sum(expo, axis=1, keepdims=True)).astype(BF16)

    def attend_values():
        attn_ref[0] = mm(probs[...], kv[:, :LATENT]).astype(BF16)

    i0 = lax.broadcasted_iota(jnp.int32, (64, 64), 0)
    i1 = lax.broadcasted_iota(jnp.int32, (64, 64), 1)
    turn = jnp.where(((i0 >> 4) == ((i1 >> 2) & 3)) & (((i0 >> 2) & 3) == (i1 >> 4)) & ((i0 & 3) == (i1 & 3)), 1.0, 0.0).astype(BF16)

    def block(p, n, size):
        return pl.ds(pl.multiple_of(n * size, size), size)

    def g2a(p):
        a1, a2, a3 = ORDERS[p]
        for step in (1, 2, 3):
            got(("s1", p, step))
        rows = mm(turn, s1[p].reshape(64, FOLD)).astype(BF16)
        own = block(p, at[a3] * 4 + at[a2], 16)
        for f in range(4):
            for t in range(5):
                tile = 5 * f + t
                for s, (off, count) in enumerate(SUBS):
                    if off <= tile < off + count:
                        xb[s][p, c, own, (tile - off) * LANE:(tile - off + 1) * LANE] = rows[16 * f:16 * f + 16, t * LANE:(t + 1) * LANE]
        for s in range(NSUB):
            ref = xb[s].at[p, c, own]
            send(("g2", p, s, 0), g2_sem, (p, s, 0), ref, ref, peer(a2, 1))
            send(("g2", p, s, 1), g2_sem, (p, s, 1), ref, ref, peer(a2, -1))

    def g2b(p, s):
        _, a2, a3 = ORDERS[p]
        way = 0 if (p + s) % 2 == 0 else 1
        got(("g2", p, s, way))
        off = -1 if way == 0 else 1
        ref = xb[s].at[p, c, block(p, at[a3] * 4 + (at[a2] + off + 4) % 4, 16)]
        send(("g2", p, s, 2), g2_sem, (p, s, 2), ref, ref, peer(a2, -off))

    def g3a(p, s):
        _, a2, a3 = ORDERS[p]
        way = 0 if (p + s) % 2 == 0 else 1
        got(("g2", p, s, 1 - way))
        got(("g2", p, s, 2))
        ref = xb[s].at[p, c, block(p, at[a3], 64)]
        send(("g3", p, s, 0), g3_sem, (p, s, 0), ref, ref, peer(a3, 1))
        send(("g3", p, s, 1), g3_sem, (p, s, 1), ref, ref, peer(a3, -1))
        send(("cx", p, s, 0), cx_sem, (p, s, 0), ref, ref, sibling)

    def g3b(p, s):
        a3 = ORDERS[p][2]
        for way, off in ((0, -1), (1, 1)):
            got(("g3", p, s, way))
            whole = (at[a3] + off + 4) % 4
            ref = xb[s].at[p, c, block(p, whole * 2 + way, 32)]
            send(("g3", p, s, 2 + way), g3_sem, (p, s, 2 + way), ref, ref, peer(a3, -off))
            ref = xb[s].at[p, c, block(p, whole, 64)]
            send(("cx", p, s, 1 + way), cx_sem, (p, s, 1 + way), ref, ref, sibling)

    def g3c(p, s):
        a3 = ORDERS[p][2]
        got(("g3", p, s, 2))
        got(("g3", p, s, 3))
        ref = xb[s].at[p, c, block(p, (at[a3] + 2) % 4, 64)]
        send(("cx", p, s, 3), cx_sem, (p, s, 3), ref, ref, sibling)

    def cxw(p, s):
        for n in range(4):
            got(("cx", p, s, n))

    def routing():
        pick = lax.broadcasted_iota(jnp.int32, (8, LANE), 1)
        pick = jnp.where((pick < 3 * EXPERTS) & ((pick & (EXPERTS - 1)) == dev), 1.0, 0.0).astype(BF16)
        weight = jnp.concatenate([nt(pick, xb[0][2, cc, :, 0:LANE]) for cc in range(2)], axis=1)
        named = weight > 0.0
        flag = jnp.where(named, 1.0, 0.0).astype(BF16)
        rows = lax.broadcasted_iota(jnp.int32, (512, 1), 0)
        cols = lax.broadcasted_iota(jnp.int32, (1, 512), 1)
        ones = lambda cond: jnp.where(cond, 1.0, 0.0).astype(BF16)
        arrival = mm(flag, ones(token_of(rows, 2) < token_of(cols, 2)))
        rank = mm(flag, ones(((rows >> 2) == (cols >> 2)) & (rows < cols)))
        limit = capacity_ref[dev].astype(F32)
        kept = jnp.where(arrival < limit, weight, 0.0)
        code = jnp.where(named, rank + 1.0, 0.0)
        for p in range(3):
            turned = code if p == 2 else mm(code.astype(BF16), ones(token_of(rows, 2) == token_of(cols, p)))
            for cc in range(2):
                slot = lax.broadcasted_iota(jnp.int32, (128, 1), 0)
                row = lax.broadcasted_iota(jnp.int32, (1, 256), 1)
                wanted = ((slot & 1) + 1).astype(F32)
                chosen = ((slot >> 1) == place_of(row, p)) & (turned[0:1, cc * 256:(cc + 1) * 256] == wanted)
                sel[p, cc] = ones(chosen)
                if p == 2:
                    kept_col[cc * 128:(cc + 1) * 128, :] = jnp.sum(
                        jnp.where(chosen, kept[0:1, cc * 256:(cc + 1) * 256], 0.0), axis=1, keepdims=True)

    def ffn(p, s):
        skip, width, start = span(p, s)
        for cc in range(2):
            packed[cc * 128:(cc + 1) * 128, :width] = mm(sel[p, cc], xb[s][p, cc, :, skip:skip + width]).astype(BF16)
        rows = packed[:, :width]
        acc_g[...] += mm(rows, gate[start:start + width, :])
        acc_u[...] += mm(rows, up[start:start + width, :])

    def act():
        g = acc_g[...]
        hidden = (g * (1.0 / (1.0 + jnp.exp(-g))) * acc_u[...] * kept_col[...]).astype(BF16)
        for p in range(3):
            for cc in range(2):
                ht[p, cc] = tn(sel[p, cc], hidden[cc * 128:(cc + 1) * 128, :]).astype(BF16)

    def c0(p, s):
        _, width, start = span(p, s)
        cs[s][p, :, :width] = mm(ht[p, 1 - c], down[:, start:start + width]).astype(BF16)
        send(("r0", p, s), r0_sem, (p, s), cs[s].at[p, :, :width], cr[s].at[p, :, :width], sibling)

    def plus(ref, rows, width, *others):
        total = ref[rows, :width].astype(F32)
        for other in others:
            total = total + other[:, :width].astype(F32)
        return total.astype(BF16)

    def a1(p, s):
        _, width, start = span(p, s)
        mine = mm(ht[p, c], down[:, start:start + width])
        got(("r0", p, s))
        cr[s][p, :, :width] = (mine + cr[s][p, :, :width].astype(F32)).astype(BF16)
        axis = ORDERS[p][2]
        k = at[axis]
        for n, (off, half, way) in enumerate(((2, 0, 1), (2, 1, -1), (1, 1, 1), (-1, 0, -1))):
            rows = block(p, ((k + off + 4) % 4) * 2 + half, 32)
            send(("r1", p, s, n), r1_sem, (p, s, n), cr[s].at[p, rows, :width], rv[s].at[p, n, :, :width], peer(axis, way))

    def a2(p, s):
        _, width, _ = span(p, s)
        axis = ORDERS[p][2]
        k = at[axis]
        for n, (off, half, way) in enumerate(((1, 0, 1), (-1, 1, -1))):
            got(("r1", p, s, n))
            rows = block(p, ((k + off + 4) % 4) * 2 + half, 32)
            t = cr[s].at[p]
            t[rows, :width] = plus(t, rows, width, rv[s].at[p, n])
            send(("r1", p, s, 4 + n), r1_sem, (p, s, 4 + n), cr[s].at[p, rows, :width], rv[s].at[p, 4 + n, :, :width], peer(axis, way))

    def b1(p, s):
        _, width, _ = span(p, s)
        k = at[ORDERS[p][2]]
        for n in (2, 3, 4, 5):
            got(("r1", p, s, n))
        t, u, v = cr[s].at[p], us[s].at[p], rv[s].at[p]
        u[0:32, :width] = plus(t, block(p, k * 2, 32), width, v.at[3], v.at[4])
        u[32:64, :width] = plus(t, block(p, k * 2 + 1, 32), width, v.at[2], v.at[5])
        axis = ORDERS[p][1]
        k = at[axis]
        way = 1 if (p + s) % 2 == 0 else -1
        for n, (off, to) in enumerate(((2, way), (-way, -way))):
            rows = block(p, (k + off + 4) % 4, 16)
            send(("r2", p, s, n), r2_sem, (p, s, n), u.at[rows, :width], rw[s].at[p, n, :, :width], peer(axis, to))

    def b2(p, s):
        _, width, _ = span(p, s)
        axis = ORDERS[p][1]
        k = at[axis]
        way = 1 if (p + s) % 2 == 0 else -1
        got(("r2", p, s, 0))
        rows = block(p, (k + way + 4) % 4, 16)
        u = us[s].at[p]
        u[rows, :width] = plus(u, rows, width, rw[s].at[p, 0])
        send(("r2", p, s, 2), r2_sem, (p, s, 2), u.at[rows, :width], rw[s].at[p, 2, :, :width], peer(axis, way))

    def b3(p, s):
        skip, width, _ = span(p, s)
        k = at[ORDERS[p][1]]
        got(("r2", p, s, 1))
        got(("r2", p, s, 2))
        total = plus(us[s].at[p], block(p, k, 16), width, rw[s].at[p, 1], rw[s].at[p, 2])
        off = SUBS[s][0]
        for t in range(width // LANE):
            tile = off + skip // LANE + t
            f, j = tile // 5, tile % 5
            vq[p, 16 * f:16 * f + 16, j * LANE:(j + 1) * LANE] = total[:, t * LANE:(t + 1) * LANE]

    def r3a(p):
        axis = ORDERS[p][0]
        d3[p] = mm(turn, vq[p]).astype(BF16)
        for step in (1, 2, 3):
            rows = block(p, (at[axis] + step) % 4, 16)
            send(("r3", p, step), r3_sem, (p, step - 1), d3.at[p, rows], r3.at[p, step - 1], peer(axis, step))

    def r3b(p):
        axis = ORDERS[p][0]
        total = d3[p, block(p, at[axis], 16), :].astype(F32)
        for step in (1, 2, 3):
            got(("r3", p, step))
            total = total + r3[p, step - 1].astype(F32)
        fold[p] = total
        for f in range(4):
            first, width = f * FOLD, min(FOLD, PART - f * FOLD)
            lead = LANE if (p == 2 and f == 0) else 0
            start = p * PART + first + lead - (LANE if p == 2 else 0)
            out_ref[:, start:start + width - lead] = fold[p, 4 * f:4 * f + 4, lead:width].astype(BF16)

    every = lambda step, *rest: [step(p, *rest) for p in range(3)]
    acc_g[...] = jnp.zeros_like(acc_g)
    acc_u[...] = jnp.zeros_like(acc_u)
    vq[...] = jnp.zeros_like(vq)
    attend_scores()
    every(g2a)
    attend_probs()
    for s in range(NSUB):
        every(g2b, s)
    for s in range(NSUB):
        every(g3a, s)
    attend_values()
    for s in range(NSUB):
        every(g3b, s)
    every(g3c, 0)
    every(cxw, 0)
    routing()
    local[2].wait()
    local[3].wait()
    every(ffn, 0)
    for s in range(1, NSUB):
        every(g3c, s)
        every(cxw, s)
        every(ffn, s)
    act()
    local[4].wait()
    stages = (c0, a1, a2, b1, b2, b3)
    lag = (0, 0, 1, 2, 3, 4)
    for tick in range(NSUB + lag[-1]):
        for stage, late in reversed(list(zip(stages, lag))):
            s = tick - late
            if 0 <= s < NSUB and stage is not c0 and stage is not a1:
                every(stage, s)
        if tick < NSUB:
            every(c0, tick)
            every(a1, tick)
    every(r3a)
    every(r3b)
    for copy in sent.values():
        copy.wait_send()


def body(moe_input, expert_ids, gate_weights, capacity, gate_proj, up_proj, down_proj, queries, latent_cache, lengths):
    vmem = pl.BlockSpec(memory_space=pltpu.VMEM)
    smem = pl.BlockSpec(memory_space=pltpu.SMEM)
    hbm = pl.BlockSpec(memory_space=pl.ANY)
    widths = [count * LANE for _, count in SUBS]
    per_sub = lambda *lead: [pltpu.VMEM(lead + (w,), BF16) for w in widths]
    dma = lambda *shape: pltpu.SemaphoreType.DMA((2,) + shape)
    scratch = [
        pltpu.VMEM((HEADS, 576), BF16), pltpu.VMEM((CACHE, 576), BF16),
        pltpu.VMEM((D, HID), BF16), pltpu.VMEM((D, HID), BF16), pltpu.VMEM((HID, D), BF16),
        pltpu.VMEM((HEADS, CACHE), F32), pltpu.VMEM((HEADS, CACHE), BF16),
        pltpu.VMEM((3, 16, FOLD), F32), pltpu.VMEM((3, 4, 16, FOLD), BF16),
        per_sub(3, 2, 256),
        pltpu.VMEM((3, 2, 128, 256), BF16), pltpu.VMEM((256, 1), F32), pltpu.VMEM((256, max(widths)), BF16),
        pltpu.VMEM((256, HID), F32), pltpu.VMEM((256, HID), F32), pltpu.VMEM((3, 2, 256, HID), BF16),
        per_sub(3, 256), per_sub(3, 256), per_sub(3, 6, 32), per_sub(3, 64), per_sub(3, 3, 16),
        pltpu.VMEM((3, 64, FOLD), BF16), pltpu.VMEM((3, 64, FOLD), BF16), pltpu.VMEM((3, 3, 16, FOLD), BF16),
        pltpu.SemaphoreType.DMA((5,)),
        dma(3, 3), dma(3, NSUB, 3), dma(3, NSUB, 4), dma(3, NSUB, 4),
        dma(3, NSUB), dma(3, NSUB, 6), dma(3, NSUB, 3), dma(3, 3),
    ]
    return pl.pallas_call(
        kernel,
        out_shape=(jax.ShapeDtypeStruct((4, D), BF16), jax.ShapeDtypeStruct((1, HEADS, LATENT), BF16)),
        in_specs=[smem, smem, vmem, vmem, vmem, hbm, hbm, hbm, hbm, hbm],
        out_specs=(vmem, vmem),
        scratch_shapes=scratch,
        compiler_params=pltpu.CompilerParams(collective_id=0, has_side_effects=True, vmem_limit_bytes=63 << 20),
        name="fused",
    )(lengths, capacity, moe_input, expert_ids, gate_weights, queries, latent_cache, gate_proj, up_proj, down_proj)


def solution(mesh):
    placed = (
        P(("sec", "dev"), None),
        P(("sec", "dev"), None),
        P(("sec", "dev"), None),
        P(),
        P("dev", None, "sec"),
        P("dev", None, "sec"),
        P("dev", "sec", None),
        P(("sec", "dev"), None, None),
        P(("sec", "dev"), None, None),
        P(("sec", "dev")),
    )
    return jax.shard_map(
        body,
        mesh=mesh,
        in_specs=placed,
        out_specs=(P(("sec", "dev"), None), P(("sec", "dev"), None, None)),
        check_vma=False,
    )
```

time: 209 us -> 85.2 us (0.41)
  blocking collectives: 120 us -> 0 us
  Pallas kernels: 0 us -> 74.5 us
  waiting for transfers between devices: 43.3 us -> 0 us
  matrix products: 14.1 us -> 0 us
  other arithmetic: 11.7 us -> 0 us
  starting transfers between devices: 6.1 us -> 0 us
  loops' own time: 2.92 us -> 0 us
    pallas_call x0 -> x1, Pallas kernels: none -> 74.5 us  [body(): pl.pallas_call(kernel, out_shape=(jax.ShapeDtypeStruct((4, D), BF16), jax...]
    unnamed x1 -> x0, blocking collectives: 68.2 us -> none
    all_to_all x1 -> x0, blocking collectives: 51.9 us -> none  [body(): lax.all_to_all(copies, ('sec', 'dev'), split_axis=0, concat_axis=0, tiled...]
    all_to_all x1 -> x0, waiting for transfers between devices: 43.3 us -> none  [body(): lax.all_to_all(partials, ('sec', 'dev'), split_axis=0, concat_axis=0, til...]
    dot_general x7 -> x0, matrix products: 14.1 us -> none  [the longest x1 5.28 us: body(): jnp.einsum('resd,edh->resh', grouped, gate_proj, preferred_element_type=j...]
    unnamed x16 -> x4, local copies, waits for them, and re-layouts: 0.32 us -> 9.08 us
    reduce_sum x5 -> x0, other arithmetic: 8.68 us -> none  [the longest x1 6.44 us: body(): jnp.sum(returned.reshape(n_sec, n_dev, per_owner, width).astype(jnp.float...]
    all_to_all x1 -> x0, starting transfers between devices: 6.1 us -> none  [body(): lax.all_to_all(partials, ('sec', 'dev'), split_axis=0, concat_axis=0, til...]
  transfers between devices with their start and end apart: 1 -> 0, of which waited for: 1 -> 0; matrix products, arithmetic and copies ran while one was open for 1% -> 0% of each run, Pallas kernels for 0% -> 0%
where the time goes in v1:
time: 85.2 us; the launch traced here: 84.9 us
  Pallas kernels  74.5 us (87%)
  local copies, waits for them, and re-layouts  9.08 us (11%)
  between operations  1.29 us (2%)
    pallas_call x1, Pallas kernels, body(): pl.pallas_call(kernel, out_shape=(jax.ShapeDtypeStruct((4, D), BF16), jax...  74.5 us
    unnamed x4, local copies, waits for them, and re-layouts  9.08 us

profile of v1, /device:TPU:0, one launch (start us, length us, event | category | flops | bytes accessed | tf_op | source)
XLA Modules:
  0.0 84.9 jit_solution(13840492140839697342)
XLA Ops:
  1.3 1.7 %copy.12.q_hbm = bf16[1,128,576]{2,1,0:T(8,128)(2,1)} copy(bf16[1,128,576]{1,2,0:T(8,128)(2,1)} %param.17) | data formatting | bytes 294912 | tf_op args[7]
  3.0 4.3 %copy.13.kv_hbm = bf16[1,2048,576]{2,1,0:T(8,128)(2,1)} copy(bf16[1,2048,576]{1,2,0:T(8,128)(2,1)} %param.18) | data formatting | bytes 4718592 | tf_op args[8]
  7.3 74.5 %fused.1 = (bf16[4,7168]{1,0:T(4,128)(2,1)}, bf16[1,128,512]{2,1,0:T(8,128)(2,1)}) custom-call(s32[1]{0:T(128)S(6)} %copy.16.lengths_ref, s32[32]{0:T(128)} %capacity_ref.1, bf16[4,7168]{1,0:T(4,128)(2,1)} %x_ref.1, s32[4,8]{1,0:T(4,128)} %ids_ref.1, f32[4,8]{1,0:T(4,128)} %gw_ref.1, bf16[1,128,576]{2,1,0:T(8,128)(2,1)} %copy.12.q_hbm, ...), custom_call_target="tpu_custom_call" | custom-call | tf_op jit(solution)/shard_map/fused/pallas_call | solution.py:412
  81.9 1.5 %copy.17 = bf16[4,7168]{1,0:T(4,128)(2,1)} copy(bf16[4,7168]{1,0:T(4,128)(2,1)} %get-tuple-element.4) | data formatting | bytes 114688
  83.3 1.6 %copy.18 = bf16[1,128,512]{2,1,0:T(8,128)(2,1)} copy(bf16[1,128,512]{2,1,0:T(8,128)(2,1)} %get-tuple-element.5) | data formatting | bytes 262144

commit v2 on v1

--- a/solution.py
+++ b/solution.py
@@ -139,8 +139,8 @@
         position = lax.broadcasted_iota(jnp.int32, (1, 512), 1)
         length = lengths_ref[0]
         for n in range(CACHE // 512):
-            rows = kv[n * 512:(n + 1) * 512, :]
-            score = nt(q[:, :LATENT], rows[:, :LATENT]) + nt(q[:, LATENT:], rows[:, LATENT:])
+            cols = kv[:, n * 512:(n + 1) * 512]
+            score = tn(q[:LATENT, :], cols[:LATENT, :]) + tn(q[LATENT:, :], cols[LATENT:, :])
             scores[:, n * 512:(n + 1) * 512] = jnp.where(position + n * 512 < length, score * SCALE, -jnp.inf)
 
     def attend_probs():
@@ -149,7 +149,7 @@
         probs[...] = (expo / jnp.sum(expo, axis=1, keepdims=True)).astype(BF16)
 
     def attend_values():
-        attn_ref[0] = mm(probs[...], kv[:, :LATENT]).astype(BF16)
+        attn_ref[0] = nt(probs[...], kv[:LATENT, :]).astype(BF16)
 
     i0 = lax.broadcasted_iota(jnp.int32, (64, 64), 0)
     i1 = lax.broadcasted_iota(jnp.int32, (64, 64), 1)
@@ -350,13 +350,13 @@
     acc_g[...] = jnp.zeros_like(acc_g)
     acc_u[...] = jnp.zeros_like(acc_u)
     vq[...] = jnp.zeros_like(vq)
-    attend_scores()
     every(g2a)
-    attend_probs()
     for s in range(NSUB):
         every(g2b, s)
     for s in range(NSUB):
         every(g3a, s)
+    attend_scores()
+    attend_probs()
     attend_values()
     for s in range(NSUB):
         every(g3b, s)
@@ -372,16 +372,13 @@
         every(ffn, s)
     act()
     local[4].wait()
-    stages = (c0, a1, a2, b1, b2, b3)
-    lag = (0, 0, 1, 2, 3, 4)
-    for tick in range(NSUB + lag[-1]):
-        for stage, late in reversed(list(zip(stages, lag))):
-            s = tick - late
-            if 0 <= s < NSUB and stage is not c0 and stage is not a1:
-                every(stage, s)
-        if tick < NSUB:
-            every(c0, tick)
-            every(a1, tick)
+    for stage in (c0, a1):
+        every(stage, 0)
+    for stage in (c0, a1):
+        every(stage, 1)
+    for stage in (a2, b1, b2, b3):
+        for s in range(NSUB):
+            every(stage, s)
     every(r3a)
     every(r3b)
     for copy in sent.values():
@@ -396,7 +393,7 @@
     per_sub = lambda *lead: [pltpu.VMEM(lead + (w,), BF16) for w in widths]
     dma = lambda *shape: pltpu.SemaphoreType.DMA((2,) + shape)
     scratch = [
-        pltpu.VMEM((HEADS, 576), BF16), pltpu.VMEM((CACHE, 576), BF16),
+        pltpu.VMEM((576, HEADS), BF16), pltpu.VMEM((576, CACHE), BF16),
         pltpu.VMEM((D, HID), BF16), pltpu.VMEM((D, HID), BF16), pltpu.VMEM((HID, D), BF16),
         pltpu.VMEM((HEADS, CACHE), F32), pltpu.VMEM((HEADS, CACHE), BF16),
         pltpu.VMEM((3, 16, FOLD), F32), pltpu.VMEM((3, 4, 16, FOLD), BF16),
@@ -417,7 +414,7 @@
         scratch_shapes=scratch,
         compiler_params=pltpu.CompilerParams(collective_id=0, has_side_effects=True, vmem_limit_bytes=63 << 20),
         name="fused",
-    )(lengths, capacity, moe_input, expert_ids, gate_weights, queries, latent_cache, gate_proj, up_proj, down_proj)
+    )(lengths, capacity, moe_input, expert_ids, gate_weights, jnp.swapaxes(queries, 1, 2), jnp.swapaxes(latent_cache, 1, 2), gate_proj, up_proj, down_proj)
 
 
 def solution(mesh):

time: 85.2 us -> 75.6 us (0.89)
  local copies, waits for them, and re-layouts: 9.08 us -> 3.03 us
  Pallas kernels: 74.5 us -> 71.1 us
    unnamed x4 -> x2, local copies, waits for them, and re-layouts: 9.08 us -> 3.03 us
    pallas_call x1, Pallas kernels: 74.5 us -> 71.1 us  [body(): pl.pallas_call(kernel, out_shape=(jax.ShapeDtypeStruct((4, D), BF16), jax...]
where the time goes in v2:
time: 75.6 us; the launch traced here: 75.4 us
  Pallas kernels  71.1 us (94%)
  local copies, waits for them, and re-layouts  3.03 us (4%)
  between operations  1.29 us (2%)
    pallas_call x1, Pallas kernels, body(): pl.pallas_call(kernel, out_shape=(jax.ShapeDtypeStruct((4, D), BF16), jax...  71.1 us
    unnamed x2, local copies, waits for them, and re-layouts  3.03 us

profile of v2, /device:TPU:0, one launch (start us, length us, event | category | flops | bytes accessed | tf_op | source)
XLA Modules:
  0.0 75.4 jit_solution(14014243325063137545)
XLA Ops:
  1.3 71.1 %fused.1 = (bf16[4,7168]{1,0:T(4,128)(2,1)}, bf16[1,128,512]{2,1,0:T(8,128)(2,1)}) custom-call(s32[1]{0:T(128)S(6)} %copy.14.lengths_ref, s32[32]{0:T(128)} %capacity_ref.1, bf16[4,7168]{1,0:T(4,128)(2,1)} %x_ref.1, s32[4,8]{1,0:T(4,128)} %ids_ref.1, f32[4,8]{1,0:T(4,128)} %gw_ref.1, bf16[1,576,128]{2,1,0:T(8,128)(2,1)} %bitcast.3, ...), custom_call_target="tpu_custom_call" | custom-call | tf_op jit(solution)/shard_map/fused/pallas_call | solution.py:409
  72.3 1.5 %copy.15 = bf16[4,7168]{1,0:T(4,128)(2,1)} copy(bf16[4,7168]{1,0:T(4,128)(2,1)} %get-tuple-element.4) | data formatting | bytes 114688
  73.8 1.6 %copy.16 = bf16[1,128,512]{2,1,0:T(8,128)(2,1)} copy(bf16[1,128,512]{2,1,0:T(8,128)(2,1)} %get-tuple-element.5) | data formatting | bytes 262144

commit v3 on v2

--- a/solution.py
+++ b/solution.py
@@ -20,7 +20,7 @@
 LANE = 128
 PART = 19 * LANE
 FOLD = 5 * LANE
-SUBS = ((0, 10), (10, 9))
+SUBS = ((0, 12), (12, 7))
 NSUB = len(SUBS)
 ORDERS = ("xyz", "yzx", "zxy")
 SCALE = 192.0 ** (-0.5)
@@ -64,8 +64,8 @@
     lengths_ref, capacity_ref, x_ref, ids_ref, gw_ref, q_hbm, kv_hbm, gate_hbm, up_hbm, down_hbm,
     out_ref, attn_ref,
     q, kv, gate, up, down, scores, probs,
-    fold, s1, xb, sel, kept_col, packed, acc_g, acc_u, ht,
-    cs, cr, rv, us, rw, vq, d3, r3,
+    fold, s1, xb, sel, sel2, kept_col, packed, acc_g, acc_u, hs, ht,
+    cs, cr, tb, rv, us, rw, vq, d3, r3,
     lsem, s1_sem, g2_sem, g3_sem, cx_sem, r0_sem, r1_sem, r2_sem, r3_sem,
 ):
     y = lax.axis_index("sec")
@@ -216,7 +216,9 @@
 
     def routing():
         pick = lax.broadcasted_iota(jnp.int32, (8, LANE), 1)
-        pick = jnp.where((pick < 3 * EXPERTS) & ((pick & (EXPERTS - 1)) == dev), 1.0, 0.0).astype(BF16)
+        which = lax.broadcasted_iota(jnp.int32, (8, LANE), 0)
+        expert = jnp.where(which == 0, dev, dev + 1 - 2 * c)
+        pick = jnp.where((pick < 3 * EXPERTS) & ((pick & (EXPERTS - 1)) == expert), 1.0, 0.0).astype(BF16)
         weight = jnp.concatenate([nt(pick, xb[0][2, cc, :, 0:LANE]) for cc in range(2)], axis=1)
         named = weight > 0.0
         flag = jnp.where(named, 1.0, 0.0).astype(BF16)
@@ -236,6 +238,8 @@
                 wanted = ((slot & 1) + 1).astype(F32)
                 chosen = ((slot >> 1) == place_of(row, p)) & (turned[0:1, cc * 256:(cc + 1) * 256] == wanted)
                 sel[p, cc] = ones(chosen)
+                other = (slot >> 1 == place_of(row, p)) & (turned[1:2, cc * 256:(cc + 1) * 256] == wanted)
+                sel2[p, cc] = ones(other)
                 if p == 2:
                     kept_col[cc * 128:(cc + 1) * 128, :] = jnp.sum(
                         jnp.where(chosen, kept[0:1, cc * 256:(cc + 1) * 256], 0.0), axis=1, keepdims=True)
@@ -251,13 +255,15 @@
     def act():
         g = acc_g[...]
         hidden = (g * (1.0 / (1.0 + jnp.exp(-g))) * acc_u[...] * kept_col[...]).astype(BF16)
+        hs[...] = hidden.reshape(2, 128, HID)
+
+    def spread():
         for p in range(3):
-            for cc in range(2):
-                ht[p, cc] = tn(sel[p, cc], hidden[cc * 128:(cc + 1) * 128, :]).astype(BF16)
+            ht[p] = tn(sel[p, c], hs[c]).astype(BF16)
 
     def c0(p, s):
         _, width, start = span(p, s)
-        cs[s][p, :, :width] = mm(ht[p, 1 - c], down[:, start:start + width]).astype(BF16)
+        cs[s][p, :, :width] = mm(hs[1 - c], down[:, start:start + width]).astype(BF16)
         send(("r0", p, s), r0_sem, (p, s), cs[s].at[p, :, :width], cr[s].at[p, :, :width], sibling)
 
     def plus(ref, rows, width, *others):
@@ -268,14 +274,14 @@
 
     def a1(p, s):
         _, width, start = span(p, s)
-        mine = mm(ht[p, c], down[:, start:start + width])
+        mine = mm(ht[p], down[:, start:start + width])
         got(("r0", p, s))
-        cr[s][p, :, :width] = (mine + cr[s][p, :, :width].astype(F32)).astype(BF16)
+        tb[s][p, :, :width] = (mine + tn(sel2[p, c], cr[s][p, :, :width])).astype(BF16)
         axis = ORDERS[p][2]
         k = at[axis]
         for n, (off, half, way) in enumerate(((2, 0, 1), (2, 1, -1), (1, 1, 1), (-1, 0, -1))):
             rows = block(p, ((k + off + 4) % 4) * 2 + half, 32)
-            send(("r1", p, s, n), r1_sem, (p, s, n), cr[s].at[p, rows, :width], rv[s].at[p, n, :, :width], peer(axis, way))
+            send(("r1", p, s, n), r1_sem, (p, s, n), tb[s].at[p, rows, :width], rv[s].at[p, n, :, :width], peer(axis, way))
 
     def a2(p, s):
         _, width, _ = span(p, s)
@@ -284,16 +290,16 @@
         for n, (off, half, way) in enumerate(((1, 0, 1), (-1, 1, -1))):
             got(("r1", p, s, n))
             rows = block(p, ((k + off + 4) % 4) * 2 + half, 32)
-            t = cr[s].at[p]
+            t = tb[s].at[p]
             t[rows, :width] = plus(t, rows, width, rv[s].at[p, n])
-            send(("r1", p, s, 4 + n), r1_sem, (p, s, 4 + n), cr[s].at[p, rows, :width], rv[s].at[p, 4 + n, :, :width], peer(axis, way))
+            send(("r1", p, s, 4 + n), r1_sem, (p, s, 4 + n), tb[s].at[p, rows, :width], rv[s].at[p, 4 + n, :, :width], peer(axis, way))
 
     def b1(p, s):
         _, width, _ = span(p, s)
         k = at[ORDERS[p][2]]
         for n in (2, 3, 4, 5):
             got(("r1", p, s, n))
-        t, u, v = cr[s].at[p], us[s].at[p], rv[s].at[p]
+        t, u, v = tb[s].at[p], us[s].at[p], rv[s].at[p]
         u[0:32, :width] = plus(t, block(p, k * 2, 32), width, v.at[3], v.at[4])
         u[32:64, :width] = plus(t, block(p, k * 2 + 1, 32), width, v.at[2], v.at[5])
         axis = ORDERS[p][1]
@@ -360,25 +366,23 @@
     attend_values()
     for s in range(NSUB):
         every(g3b, s)
-    every(g3c, 0)
+    for s in range(NSUB):
+        every(g3c, s)
     every(cxw, 0)
     routing()
     local[2].wait()
     local[3].wait()
     every(ffn, 0)
-    for s in range(1, NSUB):
-        every(g3c, s)
-        every(cxw, s)
-        every(ffn, s)
+    every(cxw, 1)
+    every(ffn, 1)
     act()
     local[4].wait()
-    for stage in (c0, a1):
+    every(c0, 1)
+    every(c0, 0)
+    spread()
+    for stage in (a1, a2, b1, b2, b3):
+        every(stage, 1)
         every(stage, 0)
-    for stage in (c0, a1):
-        every(stage, 1)
-    for stage in (a2, b1, b2, b3):
-        for s in range(NSUB):
-            every(stage, s)
     every(r3a)
     every(r3b)
     for copy in sent.values():
@@ -398,9 +402,9 @@
         pltpu.VMEM((HEADS, CACHE), F32), pltpu.VMEM((HEADS, CACHE), BF16),
         pltpu.VMEM((3, 16, FOLD), F32), pltpu.VMEM((3, 4, 16, FOLD), BF16),
         per_sub(3, 2, 256),
-        pltpu.VMEM((3, 2, 128, 256), BF16), pltpu.VMEM((256, 1), F32), pltpu.VMEM((256, max(widths)), BF16),
-        pltpu.VMEM((256, HID), F32), pltpu.VMEM((256, HID), F32), pltpu.VMEM((3, 2, 256, HID), BF16),
-        per_sub(3, 256), per_sub(3, 256), per_sub(3, 6, 32), per_sub(3, 64), per_sub(3, 3, 16),
+        pltpu.VMEM((3, 2, 128, 256), BF16), pltpu.VMEM((3, 2, 128, 256), BF16), pltpu.VMEM((256, 1), F32), pltpu.VMEM((256, max(widths)), BF16),
+        pltpu.VMEM((256, HID), F32), pltpu.VMEM((256, HID), F32), pltpu.VMEM((2, 128, HID), BF16), pltpu.VMEM((3, 256, HID), BF16),
+        per_sub(3, 128), per_sub(3, 128), per_sub(3, 256), per_sub(3, 6, 32), per_sub(3, 64), per_sub(3, 3, 16),
         pltpu.VMEM((3, 64, FOLD), BF16), pltpu.VMEM((3, 64, FOLD), BF16), pltpu.VMEM((3, 3, 16, FOLD), BF16),
         pltpu.SemaphoreType.DMA((5,)),
         dma(3, 3), dma(3, NSUB, 3), dma(3, NSUB, 4), dma(3, NSUB, 4),

time: 75.6 us -> 74.2 us (0.981)
  Pallas kernels: 71.1 us -> 69.6 us
    pallas_call x1, Pallas kernels: 71.1 us -> 69.6 us  [body(): pl.pallas_call(kernel, out_shape=(jax.ShapeDtypeStruct((4, D), BF16), jax...]
where the time goes in v3:
time: 74.2 us; the launch traced here: 74 us
  Pallas kernels  69.6 us (94%)
  local copies, waits for them, and re-layouts  3.03 us (4%)
  between operations  1.29 us (2%)
    pallas_call x1, Pallas kernels, body(): pl.pallas_call(kernel, out_shape=(jax.ShapeDtypeStruct((4, D), BF16), jax...  69.6 us
    unnamed x2, local copies, waits for them, and re-layouts  3.03 us

profile of v3, /device:TPU:0, one launch (start us, length us, event | category | flops | bytes accessed | tf_op | source)
XLA Modules:
  0.0 74.0 jit_solution(3811671707791270523)
XLA Ops:
  1.3 69.6 %fused.1 = (bf16[4,7168]{1,0:T(4,128)(2,1)}, bf16[1,128,512]{2,1,0:T(8,128)(2,1)}) custom-call(s32[1]{0:T(128)S(6)} %copy.14.lengths_ref, s32[32]{0:T(128)} %capacity_ref.1, bf16[4,7168]{1,0:T(4,128)(2,1)} %x_ref.1, s32[4,8]{1,0:T(4,128)} %ids_ref.1, f32[4,8]{1,0:T(4,128)} %gw_ref.1, bf16[1,576,128]{2,1,0:T(8,128)(2,1)} %bitcast.3, ...), custom_call_target="tpu_custom_call" | custom-call | tf_op jit(solution)/shard_map/fused/pallas_call | solution.py:413
  70.9 1.5 %copy.15 = bf16[4,7168]{1,0:T(4,128)(2,1)} copy(bf16[4,7168]{1,0:T(4,128)(2,1)} %get-tuple-element.4) | data formatting | bytes 114688
  72.4 1.6 %copy.16 = bf16[1,128,512]{2,1,0:T(8,128)(2,1)} copy(bf16[1,128,512]{2,1,0:T(8,128)(2,1)} %get-tuple-element.5) | data formatting | bytes 262144

commit v4 on v3

--- a/solution.py
+++ b/solution.py
@@ -61,9 +61,9 @@
 
 
 def kernel(
-    lengths_ref, capacity_ref, x_ref, ids_ref, gw_ref, q_hbm, kv_hbm, gate_hbm, up_hbm, down_hbm,
+    lengths_ref, capacity_ref, x_hbm, ids_hbm, gw_hbm, q_hbm, kv_hbm, gate_hbm, up_hbm, down_hbm,
     out_ref, attn_ref,
-    q, kv, gate, up, down, scores, probs,
+    x_ref, ids_ref, gw_ref, q, kv, gate, up, down, scores, probs, masks,
     fold, s1, xb, sel, sel2, kept_col, packed, acc_g, acc_u, hs, ht,
     cs, cr, tb, rv, us, rw, vq, d3, r3,
     lsem, s1_sem, g2_sem, g3_sem, cx_sem, r0_sem, r1_sem, r2_sem, r3_sem,
@@ -85,6 +85,10 @@
             pl.semaphore_signal(barrier, inc=1, device_id=peer(axis, step), device_id_type=MESH)
     pl.semaphore_signal(barrier, inc=1, device_id=sibling, device_id_type=MESH)
 
+    small = []
+    for n, (src, dst) in enumerate(((x_hbm, x_ref), (ids_hbm, ids_ref), (gw_hbm, gw_ref))):
+        small.append(pltpu.make_async_copy(src, dst, lsem.at[5 + n]))
+        small[n].start()
     local = {}
     for n, (src, dst) in enumerate(
         ((q_hbm.at[0], q), (kv_hbm.at[0], kv), (gate_hbm.at[0], gate), (up_hbm.at[0], up), (down_hbm.at[0], down))
@@ -105,6 +109,13 @@
 
     def got(key):
         sent[key].wait_recv()
+
+    for copy in small:
+        copy.wait()
+    def drain(*kinds):
+        for key, copy in sent.items():
+            if key[0] in kinds:
+                copy.wait_send()
 
     lane = lax.broadcasted_iota(jnp.int32, (4, LANE), 1)
     info = jnp.zeros((4, LANE), F32)
@@ -214,6 +225,16 @@
         for n in range(4):
             got(("cx", p, s, n))
 
+    ones = lambda cond: jnp.where(cond, 1.0, 0.0).astype(BF16)
+
+    def orders():
+        rows = lax.broadcasted_iota(jnp.int32, (512, 1), 0)
+        cols = lax.broadcasted_iota(jnp.int32, (1, 512), 1)
+        masks[0] = ones(token_of(rows, 2) == token_of(cols, 0))
+        masks[1] = ones(token_of(rows, 2) == token_of(cols, 1))
+        masks[2] = ones(token_of(rows, 2) < token_of(cols, 2))
+        masks[3] = ones(((rows >> 2) == (cols >> 2)) & (rows < cols))
+
     def routing():
         pick = lax.broadcasted_iota(jnp.int32, (8, LANE), 1)
         which = lax.broadcasted_iota(jnp.int32, (8, LANE), 0)
@@ -222,16 +243,13 @@
         weight = jnp.concatenate([nt(pick, xb[0][2, cc, :, 0:LANE]) for cc in range(2)], axis=1)
         named = weight > 0.0
         flag = jnp.where(named, 1.0, 0.0).astype(BF16)
-        rows = lax.broadcasted_iota(jnp.int32, (512, 1), 0)
-        cols = lax.broadcasted_iota(jnp.int32, (1, 512), 1)
-        ones = lambda cond: jnp.where(cond, 1.0, 0.0).astype(BF16)
-        arrival = mm(flag, ones(token_of(rows, 2) < token_of(cols, 2)))
-        rank = mm(flag, ones(((rows >> 2) == (cols >> 2)) & (rows < cols)))
+        arrival = mm(flag, masks[2])
+        rank = mm(flag, masks[3])
         limit = capacity_ref[dev].astype(F32)
         kept = jnp.where(arrival < limit, weight, 0.0)
         code = jnp.where(named, rank + 1.0, 0.0)
         for p in range(3):
-            turned = code if p == 2 else mm(code.astype(BF16), ones(token_of(rows, 2) == token_of(cols, p)))
+            turned = code if p == 2 else mm(code.astype(BF16), masks[p])
             for cc in range(2):
                 slot = lax.broadcasted_iota(jnp.int32, (128, 1), 0)
                 row = lax.broadcasted_iota(jnp.int32, (1, 256), 1)
@@ -364,6 +382,7 @@
     attend_scores()
     attend_probs()
     attend_values()
+    orders()
     for s in range(NSUB):
         every(g3b, s)
     for s in range(NSUB):
@@ -380,13 +399,27 @@
     every(c0, 1)
     every(c0, 0)
     spread()
-    for stage in (a1, a2, b1, b2, b3):
+    every(a1, 1)
+    every(a1, 0)
+    drain("s1", "g2", "g3", "cx")
+    for stage in (a2, b1, b2, b3):
         every(stage, 1)
         every(stage, 0)
     every(r3a)
+    drain("r0", "r1", "r2")
     every(r3b)
-    for copy in sent.values():
-        copy.wait_send()
+    drain("r3")
+
+
+def store(mixed, attended, mixed_out, attended_out, sem):
+    copies = [
+        pltpu.make_async_copy(mixed, mixed_out, sem.at[0]),
+        pltpu.make_async_copy(attended, attended_out, sem.at[1]),
+    ]
+    for copy in copies:
+        copy.start()
+    for copy in copies:
+        copy.wait()
 
 
 def body(moe_input, expert_ids, gate_weights, capacity, gate_proj, up_proj, down_proj, queries, latent_cache, lengths):
@@ -397,28 +430,38 @@
     per_sub = lambda *lead: [pltpu.VMEM(lead + (w,), BF16) for w in widths]
     dma = lambda *shape: pltpu.SemaphoreType.DMA((2,) + shape)
     scratch = [
+        pltpu.VMEM((4, D), BF16), pltpu.VMEM((4, TOP), jnp.int32), pltpu.VMEM((4, TOP), F32),
         pltpu.VMEM((576, HEADS), BF16), pltpu.VMEM((576, CACHE), BF16),
         pltpu.VMEM((D, HID), BF16), pltpu.VMEM((D, HID), BF16), pltpu.VMEM((HID, D), BF16),
-        pltpu.VMEM((HEADS, CACHE), F32), pltpu.VMEM((HEADS, CACHE), BF16),
+        pltpu.VMEM((HEADS, CACHE), F32), pltpu.VMEM((HEADS, CACHE), BF16), pltpu.VMEM((4, 512, 512), BF16),
         pltpu.VMEM((3, 16, FOLD), F32), pltpu.VMEM((3, 4, 16, FOLD), BF16),
         per_sub(3, 2, 256),
         pltpu.VMEM((3, 2, 128, 256), BF16), pltpu.VMEM((3, 2, 128, 256), BF16), pltpu.VMEM((256, 1), F32), pltpu.VMEM((256, max(widths)), BF16),
         pltpu.VMEM((256, HID), F32), pltpu.VMEM((256, HID), F32), pltpu.VMEM((2, 128, HID), BF16), pltpu.VMEM((3, 256, HID), BF16),
         per_sub(3, 128), per_sub(3, 128), per_sub(3, 256), per_sub(3, 6, 32), per_sub(3, 64), per_sub(3, 3, 16),
         pltpu.VMEM((3, 64, FOLD), BF16), pltpu.VMEM((3, 64, FOLD), BF16), pltpu.VMEM((3, 3, 16, FOLD), BF16),
-        pltpu.SemaphoreType.DMA((5,)),
+        pltpu.SemaphoreType.DMA((8,)),
         dma(3, 3), dma(3, NSUB, 3), dma(3, NSUB, 4), dma(3, NSUB, 4),
         dma(3, NSUB), dma(3, NSUB, 6), dma(3, NSUB, 3), dma(3, 3),
     ]
-    return pl.pallas_call(
+    mixed, attended = pl.pallas_call(
         kernel,
         out_shape=(jax.ShapeDtypeStruct((4, D), BF16), jax.ShapeDtypeStruct((1, HEADS, LATENT), BF16)),
-        in_specs=[smem, smem, vmem, vmem, vmem, hbm, hbm, hbm, hbm, hbm],
+        in_specs=[smem, smem, hbm, hbm, hbm, hbm, hbm, hbm, hbm, hbm],
         out_specs=(vmem, vmem),
         scratch_shapes=scratch,
         compiler_params=pltpu.CompilerParams(collective_id=0, has_side_effects=True, vmem_limit_bytes=63 << 20),
         name="fused",
     )(lengths, capacity, moe_input, expert_ids, gate_weights, jnp.swapaxes(queries, 1, 2), jnp.swapaxes(latent_cache, 1, 2), gate_proj, up_proj, down_proj)
+    return pl.pallas_call(
+        store,
+        out_shape=(jax.ShapeDtypeStruct((4, D), BF16), jax.ShapeDtypeStruct((1, HEADS, LATENT), BF16)),
+        in_specs=[hbm, hbm],
+        out_specs=(hbm, hbm),
+        scratch_shapes=[pltpu.SemaphoreType.DMA((2,))],
+        compiler_params=pltpu.CompilerParams(vmem_limit_bytes=62 << 20),
+        name="store",
+    )(mixed, attended)
 
 
 def solution(mesh):

time: 74.2 us -> 77.5 us (1.044)
  Pallas kernels: 69.6 us -> 76.1 us
  local copies, waits for them, and re-layouts: 3.03 us -> 0 us
    pallas_call x0 -> x1, Pallas kernels: none -> 6.83 us  [body(): pl.pallas_call(store, out_shape=(jax.ShapeDtypeStruct((4, D), BF16), jax....]
    unnamed x2 -> x0, local copies, waits for them, and re-layouts: 3.03 us -> none
where the time goes in v4:
time: 77.5 us; the launch traced here: 77.4 us
  Pallas kernels  76.1 us (98%)
  between operations  1.29 us (2%)
    pallas_call x1, Pallas kernels, body(): pl.pallas_call(kernel, out_shape=(jax.ShapeDtypeStruct((4, D), BF16), jax...  69.3 us
    pallas_call x1, Pallas kernels, body(): pl.pallas_call(store, out_shape=(jax.ShapeDtypeStruct((4, D), BF16), jax....  6.83 us

profile of v4, /device:TPU:0, one launch (start us, length us, event | category | flops | bytes accessed | tf_op | source)
XLA Modules:
  0.0 77.4 jit_solution(15517107405333193063)
XLA Ops:
  1.3 69.3 %fused.1 = (bf16[4,7168]{1,0:T(4,128)(2,1)}, bf16[1,128,512]{2,1,0:T(8,128)(2,1)}) custom-call(s32[1]{0:T(128)S(6)} %copy.12.lengths_ref, s32[32]{0:T(128)} %capacity_ref.1, bf16[4,7168]{1,0:T(4,128)(2,1)} %x_hbm.1, s32[4,8]{1,0:T(4,128)} %ids_hbm.1, f32[4,8]{1,0:T(4,128)} %gw_hbm.1, bf16[1,576,128]{2,1,0:T(8,128)(2,1)} %bitcast.3, ...), custom_call_target="tpu_custom_call" | custom-call | tf_op jit(solution)/shard_map/fused/pallas_call | solution.py:447
  70.6 6.8 %store.1 = (bf16[4,7168]{1,0:T(4,128)(2,1)}, bf16[1,128,512]{2,1,0:T(8,128)(2,1)}) custom-call(bf16[4,7168]{1,0:T(4,128)(2,1)} %get-tuple-element.4.mixed, bf16[1,128,512]{2,1,0:T(8,128)(2,1)} %get-tuple-element.5.attended), custom_call_target="tpu_custom_call" | custom-call | tf_op jit(solution)/shard_map/store/pallas_call | solution.py:456

commit v5 on v4

--- a/solution.py
+++ b/solution.py
@@ -22,6 +22,7 @@
 FOLD = 5 * LANE
 SUBS = ((0, 12), (12, 7))
 NSUB = len(SUBS)
+ROUTING = NSUB
 ORDERS = ("xyz", "yzx", "zxy")
 SCALE = 192.0 ** (-0.5)
 
@@ -169,6 +170,9 @@
     def block(p, n, size):
         return pl.ds(pl.multiple_of(n * size, size), size)
 
+    def piece(p, s):
+        return xb[s].at[0 if s == ROUTING else p]
+
     def g2a(p):
         a1, a2, a3 = ORDERS[p]
         for step in (1, 2, 3):
@@ -181,8 +185,10 @@
                 for s, (off, count) in enumerate(SUBS):
                     if off <= tile < off + count:
                         xb[s][p, c, own, (tile - off) * LANE:(tile - off + 1) * LANE] = rows[16 * f:16 * f + 16, t * LANE:(t + 1) * LANE]
-        for s in range(NSUB):
-            ref = xb[s].at[p, c, own]
+        if p == 2:
+            xb[ROUTING][0, c, own, :] = rows[0:16, 0:LANE]
+        for s in (ROUTING, *range(NSUB)) if p == 2 else range(NSUB):
+            ref = piece(p, s).at[c, own]
             send(("g2", p, s, 0), g2_sem, (p, s, 0), ref, ref, peer(a2, 1))
             send(("g2", p, s, 1), g2_sem, (p, s, 1), ref, ref, peer(a2, -1))
 
@@ -191,7 +197,7 @@
         way = 0 if (p + s) % 2 == 0 else 1
         got(("g2", p, s, way))
         off = -1 if way == 0 else 1
-        ref = xb[s].at[p, c, block(p, at[a3] * 4 + (at[a2] + off + 4) % 4, 16)]
+        ref = piece(p, s).at[c, block(p, at[a3] * 4 + (at[a2] + off + 4) % 4, 16)]
         send(("g2", p, s, 2), g2_sem, (p, s, 2), ref, ref, peer(a2, -off))
 
     def g3a(p, s):
@@ -199,7 +205,7 @@
         way = 0 if (p + s) % 2 == 0 else 1
         got(("g2", p, s, 1 - way))
         got(("g2", p, s, 2))
-        ref = xb[s].at[p, c, block(p, at[a3], 64)]
+        ref = piece(p, s).at[c, block(p, at[a3], 64)]
         send(("g3", p, s, 0), g3_sem, (p, s, 0), ref, ref, peer(a3, 1))
         send(("g3", p, s, 1), g3_sem, (p, s, 1), ref, ref, peer(a3, -1))
         send(("cx", p, s, 0), cx_sem, (p, s, 0), ref, ref, sibling)
@@ -209,16 +215,16 @@
         for way, off in ((0, -1), (1, 1)):
             got(("g3", p, s, way))
             whole = (at[a3] + off + 4) % 4
-            ref = xb[s].at[p, c, block(p, whole * 2 + way, 32)]
+            ref = piece(p, s).at[c, block(p, whole * 2 + way, 32)]
             send(("g3", p, s, 2 + way), g3_sem, (p, s, 2 + way), ref, ref, peer(a3, -off))
-            ref = xb[s].at[p, c, block(p, whole, 64)]
+            ref = piece(p, s).at[c, block(p, whole, 64)]
             send(("cx", p, s, 1 + way), cx_sem, (p, s, 1 + way), ref, ref, sibling)
 
     def g3c(p, s):
         a3 = ORDERS[p][2]
         got(("g3", p, s, 2))
         got(("g3", p, s, 3))
-        ref = xb[s].at[p, c, block(p, (at[a3] + 2) % 4, 64)]
+        ref = piece(p, s).at[c, block(p, (at[a3] + 2) % 4, 64)]
         send(("cx", p, s, 3), cx_sem, (p, s, 3), ref, ref, sibling)
 
     def cxw(p, s):
@@ -240,7 +246,7 @@
         which = lax.broadcasted_iota(jnp.int32, (8, LANE), 0)
         expert = jnp.where(which == 0, dev, dev + 1 - 2 * c)
         pick = jnp.where((pick < 3 * EXPERTS) & ((pick & (EXPERTS - 1)) == expert), 1.0, 0.0).astype(BF16)
-        weight = jnp.concatenate([nt(pick, xb[0][2, cc, :, 0:LANE]) for cc in range(2)], axis=1)
+        weight = jnp.concatenate([nt(pick, xb[ROUTING][0, cc]) for cc in range(2)], axis=1)
         named = weight > 0.0
         flag = jnp.where(named, 1.0, 0.0).astype(BF16)
         arrival = mm(flag, masks[2])
@@ -374,21 +380,27 @@
     acc_g[...] = jnp.zeros_like(acc_g)
     acc_u[...] = jnp.zeros_like(acc_u)
     vq[...] = jnp.zeros_like(vq)
-    every(g2a)
-    for s in range(NSUB):
-        every(g2b, s)
-    for s in range(NSUB):
-        every(g3a, s)
+    for p in (2, 0, 1):
+        g2a(p)
+    g2b(2, ROUTING)
+    every(g2b, 0)
+    every(g2b, 1)
+    g3a(2, ROUTING)
+    every(g3a, 0)
+    every(g3a, 1)
     attend_scores()
+    g3b(2, ROUTING)
     attend_probs()
+    g3c(2, ROUTING)
+    orders()
+    every(g3b, 0)
+    cxw(2, ROUTING)
+    routing()
+    every(g3b, 1)
     attend_values()
-    orders()
-    for s in range(NSUB):
-        every(g3b, s)
-    for s in range(NSUB):
-        every(g3c, s)
+    every(g3c, 0)
+    every(g3c, 1)
     every(cxw, 0)
-    routing()
     local[2].wait()
     local[3].wait()
     every(ffn, 0)
@@ -411,17 +423,6 @@
     drain("r3")
 
 
-def store(mixed, attended, mixed_out, attended_out, sem):
-    copies = [
-        pltpu.make_async_copy(mixed, mixed_out, sem.at[0]),
-        pltpu.make_async_copy(attended, attended_out, sem.at[1]),
-    ]
-    for copy in copies:
-        copy.start()
-    for copy in copies:
-        copy.wait()
-
-
 def body(moe_input, expert_ids, gate_weights, capacity, gate_proj, up_proj, down_proj, queries, latent_cache, lengths):
     vmem = pl.BlockSpec(memory_space=pltpu.VMEM)
     smem = pl.BlockSpec(memory_space=pltpu.SMEM)
@@ -435,16 +436,16 @@
         pltpu.VMEM((D, HID), BF16), pltpu.VMEM((D, HID), BF16), pltpu.VMEM((HID, D), BF16),
         pltpu.VMEM((HEADS, CACHE), F32), pltpu.VMEM((HEADS, CACHE), BF16), pltpu.VMEM((4, 512, 512), BF16),
         pltpu.VMEM((3, 16, FOLD), F32), pltpu.VMEM((3, 4, 16, FOLD), BF16),
-        per_sub(3, 2, 256),
+        per_sub(3, 2, 256) + [pltpu.VMEM((1, 2, 256, LANE), BF16)],
         pltpu.VMEM((3, 2, 128, 256), BF16), pltpu.VMEM((3, 2, 128, 256), BF16), pltpu.VMEM((256, 1), F32), pltpu.VMEM((256, max(widths)), BF16),
         pltpu.VMEM((256, HID), F32), pltpu.VMEM((256, HID), F32), pltpu.VMEM((2, 128, HID), BF16), pltpu.VMEM((3, 256, HID), BF16),
         per_sub(3, 128), per_sub(3, 128), per_sub(3, 256), per_sub(3, 6, 32), per_sub(3, 64), per_sub(3, 3, 16),
         pltpu.VMEM((3, 64, FOLD), BF16), pltpu.VMEM((3, 64, FOLD), BF16), pltpu.VMEM((3, 3, 16, FOLD), BF16),
         pltpu.SemaphoreType.DMA((8,)),
-        dma(3, 3), dma(3, NSUB, 3), dma(3, NSUB, 4), dma(3, NSUB, 4),
+        dma(3, 3), dma(3, NSUB + 1, 3), dma(3, NSUB + 1, 4), dma(3, NSUB + 1, 4),
         dma(3, NSUB), dma(3, NSUB, 6), dma(3, NSUB, 3), dma(3, 3),
     ]
-    mixed, attended = pl.pallas_call(
+    return pl.pallas_call(
         kernel,
         out_shape=(jax.ShapeDtypeStruct((4, D), BF16), jax.ShapeDtypeStruct((1, HEADS, LATENT), BF16)),
         in_specs=[smem, smem, hbm, hbm, hbm, hbm, hbm, hbm, hbm, hbm],
@@ -453,15 +454,6 @@
         compiler_params=pltpu.CompilerParams(collective_id=0, has_side_effects=True, vmem_limit_bytes=63 << 20),
         name="fused",
     )(lengths, capacity, moe_input, expert_ids, gate_weights, jnp.swapaxes(queries, 1, 2), jnp.swapaxes(latent_cache, 1, 2), gate_proj, up_proj, down_proj)
-    return pl.pallas_call(
-        store,
-        out_shape=(jax.ShapeDtypeStruct((4, D), BF16), jax.ShapeDtypeStruct((1, HEADS, LATENT), BF16)),
-        in_specs=[hbm, hbm],
-        out_specs=(hbm, hbm),
-        scratch_shapes=[pltpu.SemaphoreType.DMA((2,))],
-        compiler_params=pltpu.CompilerParams(vmem_limit_bytes=62 << 20),
-        name="store",
-    )(mixed, attended)
 
 
 def solution(mesh):

time: 77.5 us -> 75.6 us (0.975)
  Pallas kernels: 76.1 us -> 71.1 us
  local copies, waits for them, and re-layouts: 0 us -> 3.03 us
    pallas_call x1 -> x0, Pallas kernels: 6.83 us -> none  [body(): pl.pallas_call(store, out_shape=(jax.ShapeDtypeStruct((4, D), BF16), jax....]
    unnamed x0 -> x2, local copies, waits for them, and re-layouts: none -> 3.03 us
    pallas_call x1, Pallas kernels: 69.3 us -> 71.1 us  [body(): pl.pallas_call(kernel, out_shape=(jax.ShapeDtypeStruct((4, D), BF16), jax...]
where the time goes in v5:
time: 75.6 us; the launch traced here: 75.4 us
  Pallas kernels  71.1 us (94%)
  local copies, waits for them, and re-layouts  3.03 us (4%)
  between operations  1.29 us (2%)
    pallas_call x1, Pallas kernels, body(): pl.pallas_call(kernel, out_shape=(jax.ShapeDtypeStruct((4, D), BF16), jax...  71.1 us
    unnamed x2, local copies, waits for them, and re-layouts  3.03 us

profile of v5, /device:TPU:0, one launch (start us, length us, event | category | flops | bytes accessed | tf_op | source)
XLA Modules:
  0.0 75.4 jit_solution(1105129692615556892)
XLA Ops:
  1.3 71.1 %fused.1 = (bf16[4,7168]{1,0:T(4,128)(2,1)}, bf16[1,128,512]{2,1,0:T(8,128)(2,1)}) custom-call(s32[1]{0:T(128)S(6)} %copy.14.lengths_ref, s32[32]{0:T(128)} %capacity_ref.1, bf16[4,7168]{1,0:T(4,128)(2,1)} %x_hbm.1, s32[4,8]{1,0:T(4,128)} %ids_hbm.1, f32[4,8]{1,0:T(4,128)} %gw_hbm.1, bf16[1,576,128]{2,1,0:T(8,128)(2,1)} %bitcast.3, ...), custom_call_target="tpu_custom_call" | custom-call | tf_op jit(solution)/shard_map/fused/pallas_call | solution.py:448
  72.4 1.5 %copy.15 = bf16[4,7168]{1,0:T(4,128)(2,1)} copy(bf16[4,7168]{1,0:T(4,128)(2,1)} %get-tuple-element.4) | data formatting | bytes 114688
  73.9 1.6 %copy.16 = bf16[1,128,512]{2,1,0:T(8,128)(2,1)} copy(bf16[1,128,512]{2,1,0:T(8,128)(2,1)} %get-tuple-element.5) | data formatting | bytes 262144

commit v6 on v4

--- a/solution.py
+++ b/solution.py
@@ -374,14 +374,12 @@
     acc_g[...] = jnp.zeros_like(acc_g)
     acc_u[...] = jnp.zeros_like(acc_u)
     vq[...] = jnp.zeros_like(vq)
+    attend_scores()
     every(g2a)
     for s in range(NSUB):
         every(g2b, s)
     for s in range(NSUB):
         every(g3a, s)
-    attend_scores()
-    attend_probs()
-    attend_values()
     orders()
     for s in range(NSUB):
         every(g3b, s)
@@ -402,6 +400,8 @@
     every(a1, 1)
     every(a1, 0)
     drain("s1", "g2", "g3", "cx")
+    attend_probs()
+    attend_values()
     for stage in (a2, b1, b2, b3):
         every(stage, 1)
         every(stage, 0)
@@ -409,17 +409,6 @@
     drain("r0", "r1", "r2")
     every(r3b)
     drain("r3")
-
-
-def store(mixed, attended, mixed_out, attended_out, sem):
-    copies = [
-        pltpu.make_async_copy(mixed, mixed_out, sem.at[0]),
-        pltpu.make_async_copy(attended, attended_out, sem.at[1]),
-    ]
-    for copy in copies:
-        copy.start()
-    for copy in copies:
-        copy.wait()
 
 
 def body(moe_input, expert_ids, gate_weights, capacity, gate_proj, up_proj, down_proj, queries, latent_cache, lengths):
@@ -444,7 +433,7 @@
         dma(3, 3), dma(3, NSUB, 3), dma(3, NSUB, 4), dma(3, NSUB, 4),
         dma(3, NSUB), dma(3, NSUB, 6), dma(3, NSUB, 3), dma(3, 3),
     ]
-    mixed, attended = pl.pallas_call(
+    return pl.pallas_call(
         kernel,
         out_shape=(jax.ShapeDtypeStruct((4, D), BF16), jax.ShapeDtypeStruct((1, HEADS, LATENT), BF16)),
         in_specs=[smem, smem, hbm, hbm, hbm, hbm, hbm, hbm, hbm, hbm],
@@ -453,15 +442,6 @@
         compiler_params=pltpu.CompilerParams(collective_id=0, has_side_effects=True, vmem_limit_bytes=63 << 20),
         name="fused",
     )(lengths, capacity, moe_input, expert_ids, gate_weights, jnp.swapaxes(queries, 1, 2), jnp.swapaxes(latent_cache, 1, 2), gate_proj, up_proj, down_proj)
-    return pl.pallas_call(
-        store,
-        out_shape=(jax.ShapeDtypeStruct((4, D), BF16), jax.ShapeDtypeStruct((1, HEADS, LATENT), BF16)),
-        in_specs=[hbm, hbm],
-        out_specs=(hbm, hbm),
-        scratch_shapes=[pltpu.SemaphoreType.DMA((2,))],
-        compiler_params=pltpu.CompilerParams(vmem_limit_bytes=62 << 20),
-        name="store",
-    )(mixed, attended)
 
 
 def solution(mesh):

time: 77.5 us -> 73.8 us (0.952)
  Pallas kernels: 76.1 us -> 69.3 us
  local copies, waits for them, and re-layouts: 0 us -> 3.03 us
    pallas_call x1 -> x0, Pallas kernels: 6.83 us -> none  [body(): pl.pallas_call(store, out_shape=(jax.ShapeDtypeStruct((4, D), BF16), jax....]
    unnamed x0 -> x2, local copies, waits for them, and re-layouts: none -> 3.03 us
where the time goes in v6:
time: 73.8 us; the launch traced here: 73.6 us
  Pallas kernels  69.3 us (94%)
  local copies, waits for them, and re-layouts  3.03 us (4%)
  between operations  1.29 us (2%)
    pallas_call x1, Pallas kernels, body(): pl.pallas_call(kernel, out_shape=(jax.ShapeDtypeStruct((4, D), BF16), jax...  69.3 us
    unnamed x2, local copies, waits for them, and re-layouts  3.03 us

profile of v6, /device:TPU:0, one launch (start us, length us, event | category | flops | bytes accessed | tf_op | source)
XLA Modules:
  0.0 73.6 jit_solution(8042792506931819047)
XLA Ops:
  1.3 69.3 %fused.1 = (bf16[4,7168]{1,0:T(4,128)(2,1)}, bf16[1,128,512]{2,1,0:T(8,128)(2,1)}) custom-call(s32[1]{0:T(128)S(6)} %copy.14.lengths_ref, s32[32]{0:T(128)} %capacity_ref.1, bf16[4,7168]{1,0:T(4,128)(2,1)} %x_hbm.1, s32[4,8]{1,0:T(4,128)} %ids_hbm.1, f32[4,8]{1,0:T(4,128)} %gw_hbm.1, bf16[1,576,128]{2,1,0:T(8,128)(2,1)} %bitcast.3, ...), custom_call_target="tpu_custom_call" | custom-call | tf_op jit(solution)/shard_map/fused/pallas_call | solution.py:436
  70.6 1.5 %copy.15 = bf16[4,7168]{1,0:T(4,128)(2,1)} copy(bf16[4,7168]{1,0:T(4,128)(2,1)} %get-tuple-element.4) | data formatting | bytes 114688
  72.0 1.6 %copy.16 = bf16[1,128,512]{2,1,0:T(8,128)(2,1)} copy(bf16[1,128,512]{2,1,0:T(8,128)(2,1)} %get-tuple-element.5) | data formatting | bytes 262144
